TPU v7x, 512 devices: a whole 4x4x16 slice. The times are simulated.
512 devices in a mesh: inner: 16 (over z_hi, x, core), outer: 32 (over z_lo, y).
Axes of the slice: x: 4, y: 4, z: 16 (z_hi: 2, z_lo: 8; z = z_hi * 8 + z_lo), core: 2. Of those that a mesh axis runs over, the one named last changes fastest.
Arguments:
- centres: float32 [3, 262144], P(None, ('outer', 'inner')), may hold values from -1 to 1
- leaf_order: int32 [512, 512], P(('outer', 'inner')), may hold values from 0 to 511, each once within a row
- nugget: float32 [262144], P(('outer', 'inner')), may hold values from 0.5 to 2
- left_fine: bfloat16 [4, 64, 262144], P(None, None, ('outer', 'inner')), may hold values from -0.75 to 0.75
- right_fine: bfloat16 [4, 64, 262144], P(None, None, ('outer', 'inner')), may hold values from -0.133466405 to 0.133466405
- left_coarse: bfloat16 [5, 64, 262144], P(None, None, ('outer', 'inner')), may hold values from -0.75 to 0.75
- right_coarse: bfloat16 [5, 64, 262144], P(None, None, ('outer', 'inner')), may hold values from -0.033366601 to 0.033366601
- right_sides: float32 [48, 262144], P(None, ('outer', 'inner')), may hold values from -320 to 320
Outputs:
- next_basis: float32 [48, 262144], P(None, ('outer', 'inner'))
- hessenberg: float32 [48, 5, 4], replicated
Inputs may be any that keep to these rules, and one draw needn't show every extreme that they name: `leaf_order`: each row is an order of 0 to 511, each number once.
All inputs are finite; a program needn't handle non-finite values.
Results may differ from a plain program's by a relative error of at most 0.0037.
Values sent between devices are 32-bit elements; how exact they have to be, the bound alone decides.
A program may use at most 64 MiB of HBM per device.

v0:
```python
import jax
import jax.numpy as jnp
from jax import lax
from jax.sharding import PartitionSpec as P

ROWS = 512
STEPS = 4


SHAPE_SQUARED = 0.0625
EPSILON = 1e-06


def partner(value, axis, stride):
    return lax.ppermute(value, axis, [(i, i ^ 1 << stride) for i in range(lax.axis_size(axis))])


def kernel_rows(points, count):
    distance = jnp.zeros((count, points.shape[1]), jnp.float32)
    for coord in range(3):
        between = points[coord][:, None] - points[coord][None, :]
        distance = distance + between * between
    return (jnp.sqrt(distance + SHAPE_SQUARED) / jnp.sqrt(jnp.float32(ROWS))).astype(jnp.bfloat16)


def on_device(
    centres, leaf_order, nugget, left_fine, right_fine, left_coarse, right_coarse, right_sides
):
    rows = right_sides.shape[1]
    nrhs_count = right_sides.shape[0]
    rank_count = left_fine.shape[1]
    fine_count = left_fine.shape[0]
    coarse_count = left_coarse.shape[0]
    points = jnp.take(centres, leaf_order[0], axis=1)
    step_rows = 512
    starts = jnp.arange(rows // step_rows, dtype=jnp.int32) * step_rows

    def kernel_piece(offset):
        return kernel_rows(points, step_rows)

    kernel = lax.map(kernel_piece, starts).reshape(rows, rows)
    total = jnp.float32(rows * lax.axis_size("inner") * lax.axis_size("outer"))
    start = lax.psum(jnp.sum(right_sides * right_sides, axis=1), ("inner", "outer")) / total
    basis = [right_sides / jnp.sqrt(start + EPSILON)[:, None]]
    columns = []
    for step_index in range(STEPS):
        vector = basis[-1]
        rounded = vector.astype(jnp.bfloat16)
        fine_terms = jnp.einsum(
            "lkr,nr->lkn", right_fine, rounded, preferred_element_type=jnp.float32
        ).reshape(fine_count, -1)
        coarse_terms = jnp.einsum(
            "lkr,nr->lkn", right_coarse, rounded, preferred_element_type=jnp.float32
        ).reshape(coarse_count, -1)
        fine_acc = fine_terms
        coarse_acc = coarse_terms
        fine_list = []
        for bit_index in range(fine_count):
            recv_fine, recv_coarse = partner((fine_acc[bit_index:], coarse_acc), "inner", bit_index)
            fine_list.append(recv_fine[0])
            fine_acc = jnp.concatenate(
                [fine_acc[: bit_index + 1], fine_acc[bit_index + 1 :] + recv_fine[1:]], 0
            )
            coarse_acc = coarse_acc + recv_coarse
        coarse_list = []
        for bit_index in range(coarse_count):
            received = partner(coarse_acc[bit_index:], "outer", bit_index)
            coarse_list.append(received[0])
            coarse_acc = jnp.concatenate(
                [coarse_acc[: bit_index + 1], coarse_acc[bit_index + 1 :] + received[1:]], 0
            )
        sibling_fine = jnp.stack(fine_list, 0)
        sibling_coarse = jnp.stack(coarse_list, 0)
        result = nugget[None, :] * vector + jnp.dot(
            rounded, kernel, preferred_element_type=jnp.float32
        )
        fine_sums = sibling_fine.reshape(fine_count, rank_count, nrhs_count)
        coarse_sums = sibling_coarse.reshape(coarse_count, rank_count, nrhs_count)
        result = result + jnp.einsum(
            "lkn,lkr->nr", fine_sums, left_fine.astype(jnp.float32), precision=lax.Precision.HIGHEST
        )
        result = result + jnp.einsum(
            "lkn,lkr->nr",
            coarse_sums,
            left_coarse.astype(jnp.float32),
            precision=lax.Precision.HIGHEST,
        )
        image = result
        local_products = jnp.stack([jnp.sum(earlier * image, axis=1) for earlier in basis])
        coeffs = lax.psum(local_products, ("inner", "outer")) / total
        for position, earlier in enumerate(basis):
            image = image - coeffs[position][:, None] * earlier
        squares = lax.psum(jnp.sum(image * image, axis=1), ("inner", "outer")) / total
        norm_value = jnp.sqrt(squares + EPSILON)
        column = jnp.concatenate(
            [
                coeffs,
                norm_value[None],
                jnp.zeros((STEPS - 1 - step_index, nrhs_count), jnp.float32),
            ],
            0,
        )
        columns.append(column)
        basis.append(image / norm_value[:, None])
    hessenberg = jnp.transpose(jnp.stack(columns, 0), (2, 1, 0))
    return (basis[-1], hessenberg)


def solution(mesh):
    return jax.shard_map(
        on_device,
        mesh=mesh,
        in_specs=(
            P(None, ("outer", "inner")),
            P(("outer", "inner"), None),
            P(("outer", "inner")),
            P(None, None, ("outer", "inner")),
            P(None, None, ("outer", "inner")),
            P(None, None, ("outer", "inner")),
            P(None, None, ("outer", "inner")),
            P(None, ("outer", "inner")),
        ),
        out_specs=(P(None, ("outer", "inner")), P()),
        check_vma=False,
    )
```

profile of v0, /device:TPU:1, one launch (start us, length us, event | category | flops | bytes accessed | tf_op | source)
XLA Modules:
  0.0 1235.6 jit_solution(7930557198719599898)
XLA Ops:
  1.7 111.1 %psum.63 = f32[48]{0:T(128)S(1)} all-reduce(f32[48]{0:T(128)S(1)} %multiply_reduce_fusion.14), channel_id=1, replica_groups=mesh['inner'=16,'outer'=32] {'inner','outer'}, use_global_device_ids=true, to_apply=%region_1.2 | all-reduce | flops 48 | bytes 384 | tf_op jit(solution)/shard_map/psum | solution.py:43
  122.9 3.7 collective-permute-done.5
  126.6 2.9 collective-permute-start.6
  129.9 3.5 collective-permute-done.6
  133.4 7.1 collective-permute-start.7
  142.5 6.4 collective-permute-done.7
  163.5 10.9 collective-permute-start.3
  176.9 3.1 collective-permute-done.11
  180.0 3.2 collective-permute-start.12
  183.6 4.9 collective-permute-done.12
  189.2 106.7 %psum.64 = f32[1,48]{1,0:T(1,128)S(1)} all-reduce(f32[1,48]{1,0:T(1,128)S(1)} %bitcast.151), channel_id=1, replica_groups=mesh['inner'=16,'outer'=32] {'inner','outer'}, use_global_device_ids=true, to_apply=%region_3.4 | all-reduce | flops 48 | bytes 384 | tf_op jit(solution)/shard_map/psum | solution.py:90
  296.1 99.6 %psum.65 = f32[48]{0:T(128)S(1)} all-reduce(f32[48]{0:T(128)S(1)} %multiply_reduce_fusion.12), channel_id=1, replica_groups=mesh['inner'=16,'outer'=32] {'inner','outer'}, use_global_device_ids=true, to_apply=%region_5.6 | all-reduce | flops 48 | bytes 384 | tf_op jit(solution)/shard_map/psum | solution.py:93
  402.9 3.0 collective-permute-done.18
  406.0 4.1 collective-permute-start.19
  410.6 3.1 collective-permute-start.13
  413.6 6.5 collective-permute-start.20
  421.3 12.2 collective-permute-done.20
  439.0 3.0 collective-permute-start.22
  442.1 5.9 collective-permute-start.15
  450.0 6.8 collective-permute-start.16
  458.8 4.4 collective-permute-done.16
  466.0 5.7 collective-permute-done.25
  472.5 103.5 %psum.66 = f32[2,48]{1,0:T(2,128)S(1)} all-reduce(f32[2,48]{1,0:T(2,128)S(1)} %pad_maximum_fusion.6), channel_id=1, replica_groups=mesh['inner'=16,'outer'=32] {'inner','outer'}, use_global_device_ids=true, to_apply=%region_8.9 | all-reduce | flops 96 | bytes 768 | tf_op jit(solution)/shard_map/psum | solution.py:90
  576.1 99.6 %psum.67 = f32[48]{0:T(128)S(1)} all-reduce(f32[48]{0:T(128)S(1)} %get-tuple-element.31), channel_id=1, replica_groups=mesh['inner'=16,'outer'=32] {'inner','outer'}, use_global_device_ids=true, to_apply=%region_10.11 | all-reduce | flops 48 | bytes 384 | tf_op jit(solution)/shard_map/psum | solution.py:93
  682.2 3.6 collective-permute-done.31
  685.7 3.4 collective-permute-start.32
  689.6 3.2 collective-permute-start.26
  692.9 6.4 collective-permute-start.33
  700.5 11.8 collective-permute-done.33
  717.7 3.0 collective-permute-start.35
  720.8 5.0 collective-permute-start.28
  728.0 7.4 collective-permute-start.29
  737.4 3.8 collective-permute-done.29
  744.8 5.1 collective-permute-done.38
  750.7 104.0 %psum.68 = f32[3,48]{1,0:T(4,128)S(1)} all-reduce(f32[3,48]{1,0:T(4,128)S(1)} %pad_maximum_fusion.4), channel_id=1, replica_groups=mesh['inner'=16,'outer'=32] {'inner','outer'}, use_global_device_ids=true, to_apply=%region_14.15 | all-reduce | flops 144 | bytes 1152 | tf_op jit(solution)/shard_map/psum | solution.py:90
  854.9 99.2 %psum.69 = f32[48]{0:T(128)S(1)} all-reduce(f32[48]{0:T(128)S(1)} %get-tuple-element.29), channel_id=1, replica_groups=mesh['inner'=16,'outer'=32] {'inner','outer'}, use_global_device_ids=true, to_apply=%region_16.17 | all-reduce | flops 48 | bytes 384 | tf_op jit(solution)/shard_map/psum | solution.py:93
  961.0 3.2 collective-permute-done.44
  964.2 3.8 collective-permute-start.45
  969.1 3.1 collective-permute-start.39
  972.2 6.7 collective-permute-start.46
  979.2 12.9 %collective-permute-done.46 = f32[5,3072]{1,0:T(8,128)S(1)} collective-permute-done((f32[5,3072]{1,0:T(8,128)S(1)}, f32[5,3072]{1,0:T(8,128)S(1)}, u32[]{:S(2)}, u32[]{:S(2)}) %collective-permute-start.46) | collective-permute-done | bytes 61472 | tf_op jit(solution)/shard_map/ppermute | solution.py:15
  994.6 3.5 collective-permute-start.40
  1000.1 6.6 collective-permute-start.41
  1008.8 6.8 collective-permute-start.42
  1017.5 4.5 collective-permute-done.42
  1025.0 5.6 collective-permute-done.51
  1031.4 103.2 %psum.70 = f32[4,48]{1,0:T(4,128)S(1)} all-reduce(f32[4,48]{1,0:T(4,128)S(1)} %pad_maximum_fusion.5), channel_id=1, replica_groups=mesh['inner'=16,'outer'=32] {'inner','outer'}, use_global_device_ids=true, to_apply=%region_21.22 | all-reduce | flops 192 | bytes 1536 | tf_op jit(solution)/shard_map/psum | solution.py:90
  1134.8 99.4 %psum.71 = f32[48]{0:T(128)S(1)} all-reduce(f32[48]{0:T(128)S(1)} %get-tuple-element.27), channel_id=1, replica_groups=mesh['inner'=16,'outer'=32] {'inner','outer'}, use_global_device_ids=true, to_apply=%region_23.24 | all-reduce | flops 48 | bytes 384 | tf_op jit(solution)/shard_map/psum | solution.py:93
  (297 shorter events, 97.2 us)
Async XLA Ops:
  114.2 36.5 %collective-permute-start = (f32[4,3072]{1,0:T(4,128)S(1)}, f32[4,3072]{1,0:T(4,128)S(1)}, u32[]{:S(2)}, u32[]{:S(2)}) collective-permute-start(f32[4,3072]{1,0:T(4,128)S(1)} %reshape.111), channel_id=1, source_target_pairs={{0,32},{32,0},{64,96},{96,64},{128,160},{160,128},{192,224},{224,1... | collective-permute-start | bytes 147464 | tf_op jit(solution)/shard_map/ppermute | solution.py:15
  120.8 5.8 collective-permute-start.5
  126.6 6.9 collective-permute-start.6
  133.4 15.4 %collective-permute-start.7 = (f32[5,3072]{1,0:T(8,128)S(1)}, f32[5,3072]{1,0:T(8,128)S(1)}, u32[]{:S(2)}, u32[]{:S(2)}) collective-permute-start(f32[5,3072]{1,0:T(8,128)S(1)} %add.251), channel_id=1, source_target_pairs={{0,256},{32,288},{64,320},{96,352},{128,384},{160,416},{192,448},{... | collective-permute-start | bytes 184328 | tf_op jit(solution)/shard_map/ppermute | solution.py:15
  148.8 5.7 collective-permute-start.8
  150.8 6.6 collective-permute-start.1
  154.5 6.3 collective-permute-start.9
  157.4 6.1 collective-permute-start.2
  160.9 13.6 %collective-permute-start.10 = (f32[3,3072]{1,0:T(4,128)S(1)}, f32[3,3072]{1,0:T(4,128)S(1)}, u32[]{:S(2)}, u32[]{:S(2)}) collective-permute-start(f32[3,3072]{1,0:T(4,128)S(1)} %slice_add_fusion.9), channel_id=1, source_target_pairs={{0,4},{1,5},{2,6},{3,7},{4,0},{5,1},{6,2},{7,3},{8,12},{9,13},{10,... | collective-permute-start | bytes 110600 | tf_op jit(solution)/shard_map/ppermute | solution.py:15
  163.5 13.2 %collective-permute-start.3 = (f32[1,3072]{1,0:T(1,128)S(1)}, f32[1,3072]{1,0:T(1,128)S(1)}, u32[]{:S(2)}, u32[]{:S(2)}) collective-permute-start(f32[1,3072]{1,0:T(1,128)S(1)} %get-tuple-element.48), channel_id=1, source_target_pairs={{0,256},{32,288},{64,320},{96,352},{128,384},{160,416},{192,448},{... | collective-permute-start | bytes 36872 | tf_op jit(solution)/shard_map/ppermute | solution.py:15
  174.5 5.5 collective-permute-start.11
  180.0 8.5 collective-permute-start.12
  400.0 5.9 collective-permute-start.18
  406.0 7.7 collective-permute-start.19
  410.6 25.4 %collective-permute-start.13 = (f32[4,3072]{1,0:T(4,128)S(1)}, f32[4,3072]{1,0:T(4,128)S(1)}, u32[]{:S(2)}, u32[]{:S(2)}) collective-permute-start(f32[4,3072]{1,0:T(4,128)S(1)} %reshape.115), channel_id=1, source_target_pairs={{0,32},{32,0},{64,96},{96,64},{128,160},{160,128},{192,224},{224,1... | collective-permute-start | bytes 147464 | tf_op jit(solution)/shard_map/ppermute | solution.py:15
  413.6 19.9 %collective-permute-start.20 = (f32[5,3072]{1,0:T(8,128)S(1)}, f32[5,3072]{1,0:T(8,128)S(1)}, u32[]{:S(2)}, u32[]{:S(2)}) collective-permute-start(f32[5,3072]{1,0:T(8,128)S(1)} %add.266), channel_id=1, source_target_pairs={{0,256},{32,288},{64,320},{96,352},{128,384},{160,416},{192,448},{... | collective-permute-start | bytes 184328 | tf_op jit(solution)/shard_map/ppermute | solution.py:15
  433.6 5.4 collective-permute-start.21
  436.0 6.1 collective-permute-start.14
  439.0 9.0 collective-permute-start.22
  442.1 7.9 collective-permute-start.15
  448.0 8.8 collective-permute-start.23
  450.0 13.2 %collective-permute-start.16 = (f32[1,3072]{1,0:T(1,128)S(1)}, f32[1,3072]{1,0:T(1,128)S(1)}, u32[]{:S(2)}, u32[]{:S(2)}) collective-permute-start(f32[1,3072]{1,0:T(1,128)S(1)} %get-tuple-element.44), channel_id=1, source_target_pairs={{0,256},{32,288},{64,320},{96,352},{128,384},{160,416},{192,448},{... | collective-permute-start | bytes 36872 | tf_op jit(solution)/shard_map/ppermute | solution.py:15
  456.8 6.5 collective-permute-start.24
  463.4 8.3 collective-permute-start.25
  679.8 5.9 collective-permute-start.31
  685.7 7.1 collective-permute-start.32
  689.6 25.4 %collective-permute-start.26 = (f32[4,3072]{1,0:T(4,128)S(1)}, f32[4,3072]{1,0:T(4,128)S(1)}, u32[]{:S(2)}, u32[]{:S(2)}) collective-permute-start(f32[4,3072]{1,0:T(4,128)S(1)} %reshape.119), channel_id=1, source_target_pairs={{0,32},{32,0},{64,96},{96,64},{128,160},{160,128},{192,224},{224,1... | collective-permute-start | bytes 147464 | tf_op jit(solution)/shard_map/ppermute | solution.py:15
  692.9 19.4 %collective-permute-start.33 = (f32[5,3072]{1,0:T(8,128)S(1)}, f32[5,3072]{1,0:T(8,128)S(1)}, u32[]{:S(2)}, u32[]{:S(2)}) collective-permute-start(f32[5,3072]{1,0:T(8,128)S(1)} %add.281), channel_id=1, source_target_pairs={{0,256},{32,288},{64,320},{96,352},{128,384},{160,416},{192,448},{... | collective-permute-start | bytes 184328 | tf_op jit(solution)/shard_map/ppermute | solution.py:15
  712.3 5.4 collective-permute-start.34
  715.0 5.7 collective-permute-start.27
  717.7 8.1 collective-permute-start.35
  720.8 7.2 collective-permute-start.28
  725.9 9.6 collective-permute-start.36
  728.0 13.2 %collective-permute-start.29 = (f32[1,3072]{1,0:T(1,128)S(1)}, f32[1,3072]{1,0:T(1,128)S(1)}, u32[]{:S(2)}, u32[]{:S(2)}) collective-permute-start(f32[1,3072]{1,0:T(1,128)S(1)} %get-tuple-element.40), channel_id=1, source_target_pairs={{0,256},{32,288},{64,320},{96,352},{128,384},{160,416},{192,448},{... | collective-permute-start | bytes 36872 | tf_op jit(solution)/shard_map/ppermute | solution.py:15
  735.5 6.1 collective-permute-start.37
  741.6 8.3 collective-permute-start.38
  958.2 5.9 collective-permute-start.44
  964.2 8.0 collective-permute-start.45
  969.1 25.4 %collective-permute-start.39 = (f32[4,3072]{1,0:T(4,128)S(1)}, f32[4,3072]{1,0:T(4,128)S(1)}, u32[]{:S(2)}, u32[]{:S(2)}) collective-permute-start(f32[4,3072]{1,0:T(4,128)S(1)} %reshape.123), channel_id=1, source_target_pairs={{0,32},{32,0},{64,96},{96,64},{128,160},{160,128},{192,224},{224,1... | collective-permute-start | bytes 147464 | tf_op jit(solution)/shard_map/ppermute | solution.py:15
  972.2 19.8 %collective-permute-start.46 = (f32[5,3072]{1,0:T(8,128)S(1)}, f32[5,3072]{1,0:T(8,128)S(1)}, u32[]{:S(2)}, u32[]{:S(2)}) collective-permute-start(f32[5,3072]{1,0:T(8,128)S(1)} %add.296), channel_id=1, source_target_pairs={{0,256},{32,288},{64,320},{96,352},{128,384},{160,416},{192,448},{... | collective-permute-start | bytes 184328 | tf_op jit(solution)/shard_map/ppermute | solution.py:15
  992.1 6.0 collective-permute-start.47
  994.6 5.5 collective-permute-start.40
  998.1 8.6 collective-permute-start.48
  1000.1 8.6 collective-permute-start.41
  1006.8 8.8 collective-permute-start.49
  1008.8 13.3 %collective-permute-start.42 = (f32[1,3072]{1,0:T(1,128)S(1)}, f32[1,3072]{1,0:T(1,128)S(1)}, u32[]{:S(2)}, u32[]{:S(2)}) collective-permute-start(f32[1,3072]{1,0:T(1,128)S(1)} %get-tuple-element.36), channel_id=1, source_target_pairs={{0,256},{32,288},{64,320},{96,352},{128,384},{160,416},{192,448},{... | collective-permute-start | bytes 36872 | tf_op jit(solution)/shard_map/ppermute | solution.py:15
  1015.6 6.6 collective-permute-start.50
  1022.3 8.4 collective-permute-start.51
  (44 other events, 731.4 us)
where the time goes:
time: 1240 us
  blocking collectives  926 us (75%)
  starting transfers between devices  182 us (15%)
  waiting for transfers between devices  103 us (8%)
    psum x4, blocking collectives, on_device(): coeffs = lax.psum(local_products, ('inner', 'outer')) / total  417 us
    psum x4, blocking collectives, on_device(): lax.psum(jnp.sum(image * image, axis=1), ('inner', 'outer')) / total  398 us
    ppermute x52, starting transfers between devices, partner(): lax.ppermute(value, axis, [(i, i ^ 1 << stride) for i in range(lax.axis_s...  182 us
    psum x1, blocking collectives, on_device(): lax.psum(jnp.sum(right_sides * right_sides, axis=1), ('inner', 'outer'))  111 us
    ppermute x52, waiting for transfers between devices, partner(): lax.ppermute(value, axis, [(i, i ^ 1 << stride) for i in range(lax.axis_s...  103 us
  transfers between devices with their start and end apart: 52, of which 26 were waited for; matrix products, arithmetic and copies ran while one was open for 1% of the time, Pallas kernels for 0%

commit v1 on v0

v1 whole, which is shorter than its diff:
```python
import functools

import jax
import jax.numpy as jnp
from jax import lax
from jax.experimental import pallas as pl
from jax.experimental.pallas import tpu as pltpu
from jax.sharding import PartitionSpec as P

ROWS = 512
RANK = 64
NRHS = 48
STEPS = 4
SLICES = 32
DEPTH = 16
TOTAL = 262144.0
SHAPE_SQUARED = 0.0625
EPSILON = 1e-06
MESH = pl.DeviceIdType.MESH
F32 = jnp.float32
BF16 = jnp.bfloat16


def split(value):
    high = value.astype(BF16)
    low = (value - high.astype(F32)).astype(BF16)
    return jnp.concatenate([high, low], 0)


def joined(value):
    return value[:NRHS] + value[NRHS:]


def dot(left, right):
    return jnp.dot(left, right, preferred_element_type=F32)


def dot_t(left, right):
    return lax.dot_general(left, right, (((1,), (1,)), ((), ())), preferred_element_type=F32)


def total_of(value):
    return jnp.sum(value, axis=1, keepdims=True)


def tree(values):
    values = list(values)
    while len(values) > 1:
        values = [values[i] + values[i + 1] for i in range(0, len(values), 2)]
    return values[0]


def body(
    centres, leaf_order, nugget, left_fine, right_fine, left_coarse, right_coarse, right_sides,
    out, hess,
    c8, order_right, order_left, kernel, tx0, rx0, tx1, rx1, tx2, rx2, txp, rxp, tx3, rx3,
    tx4, rx4, tx5, rx5, send, recv,
):
    inner, outer = lax.axis_index("inner"), lax.axis_index("outer")
    plane = (outer % 4) * 8 + inner % 8

    def plane_peer(d):
        return {"inner": inner ^ (d & 7), "outer": outer ^ (d >> 3)}

    def depth_peer(z):
        return {"inner": inner ^ ((z & 1) << 3), "outer": outer ^ ((z >> 1) << 2)}

    def copy(src, dst, sems, peer):
        return pltpu.make_async_remote_copy(
            src_ref=src, dst_ref=dst, send_sem=send.at[sems], recv_sem=recv.at[sems],
            device_id=peer, device_id_type=MESH,
        )

    barrier = pltpu.get_barrier_semaphore()

    @pl.loop(1, SLICES)
    def _(d):
        pl.semaphore_signal(barrier, inc=1, device_id=plane_peer(d), device_id_type=MESH)

    @pl.loop(1, DEPTH)
    def _(z):
        pl.semaphore_signal(barrier, inc=1, device_id=depth_peer(z), device_id_type=MESH)

    row = lax.broadcasted_iota(jnp.int32, (512, 512), 0)
    col = lax.broadcasted_iota(jnp.int32, (512, 512), 1)
    wanted = (row & 7) * RANK + ((row & 255) >> 3) * 2 + (row >> 8)
    order = jnp.where(wanted == col, 1.0, 0.0).astype(BF16)

    def levels_above(fine, coarse):
        return jnp.concatenate(
            [fine[1:].reshape(3 * RANK, ROWS), coarse[...].reshape(5 * RANK, ROWS)], 0
        )

    order_right[...] = dot(order, levels_above(right_fine, right_coarse)).astype(BF16)

    lane = lax.broadcasted_iota(jnp.int32, (32, 256), 1)
    spare_dot, spare_odd = (lane >> 4) & 7, ((lane >> 3) & 1) == 1
    tile_row = lax.broadcasted_iota(jnp.int32, (8, 128), 0)
    tile_spare = lax.broadcasted_iota(jnp.int32, (8, 128), 1) >= 96

    def start_round(r, vector, dots):
        parts = split(vector)
        terms = joined(dot_t(parts, order_right[...]))
        spare = jnp.zeros((32, 256), F32)
        for i, value in enumerate(dots):
            spare = jnp.where(
                spare_dot == i, jnp.where(spare_odd, value[16:48], value[0:32]), spare
            )
        tiles = jnp.concatenate([terms[:, :256], terms[:, 256:], spare], 0).T
        tx1[r] = tiles.reshape(SLICES, 8, 128)
        if r == 0:
            pl.semaphore_wait(barrier, SLICES + DEPTH - 2)

        @pl.loop(1, SLICES)
        def _(d):
            copy(tx1.at[r, plane ^ d], rx1.at[r, d], (r, 1), plane_peer(d)).start()

        tx0[r] = joined(dot_t(parts, right_fine[0]))
        copy(tx0.at[r], rx0.at[r], (r, 0), plane_peer(1)).start()
        return parts

    def sums_round(r):
        copy(tx1.at[r, pl.ds(1, 31)], rx1.at[r, pl.ds(1, 31)], (r, 1), plane_peer(1)).wait_recv()
        own = tx1[r, plane]
        chip = [own + rx1[r, 1]] + [rx1[r, 2 * e] + rx1[r, 2 * e + 1] for e in range(1, 16)]
        pair = [chip[2 * h] + chip[2 * h + 1] for h in range(8)]
        line = [pair[2 * y] + pair[2 * y + 1] for y in range(4)]
        half = [line[0] + line[1], line[2] + line[3]]
        whole = half[0] + half[1]
        for z in range(3):
            tx2[r, z] = whole[5 + z : 6 + z]
        for m in range(2):
            txp[r, m] = jnp.where(
                tile_row < 5, line[2 * m], pltpu.roll(line[2 * m + 1], 3, axis=0)
            )
        copy(txp.at[r], rxp.at[r], (r, 3), depth_peer(1)).start()

        @pl.loop(2, DEPTH)
        def _(z):
            which = jnp.where(z < 4, 0, jnp.where(z < 8, 1, 2))
            copy(tx2.at[r, which], rx2.at[r, z], (r, 2), depth_peer(z)).start()

        copy(txp.at[r], rxp.at[r], (r, 3), depth_peer(1)).wait_recv()
        rows = rx2.at[r, pl.ds(2, 14)]
        copy(rows, rows, (r, 2), depth_peer(1)).wait_recv()
        far = []
        for m in range(2):
            both = rxp[r, m]
            far += [both, pltpu.roll(both, 5, axis=0)]
        far_half = [far[0] + far[1], far[2] + far[3]]
        six = tree([rx2[r, z] for z in range(2, 4)])
        seven = tree([rx2[r, z] for z in range(4, 8)])
        eight = tree([rx2[r, z] for z in range(8, 16)])
        products = whole[2:3] + (far_half[0] + far_half[1])[2:3]
        products = products + six + seven + eight
        high = jnp.where(tile_row == 5, six, jnp.where(tile_row == 6, seven, eight))
        for y in range(4):
            base = jnp.where(tile_row == 4, half[1 - y // 2] + far_half[1 - y // 2], high)
            base = jnp.where(tile_row == 3, line[y ^ 1] + far[y ^ 1], base)
            base = jnp.where(tile_row == 2, far[y], base)
            for x in range(4):
                e = 4 * y + x
                tile = jnp.where(tile_row == 1, pair[(e // 2) ^ 1], base)
                tile = jnp.where(tile_row == 0, chip[e ^ 1], tile)
                tile = jnp.where(tile_spare, products, tile)
                tx3[r, e] = tile
                if e == 0:
                    rx3[r, plane] = tile

        @pl.loop(1, SLICES)
        def _(d):
            copy(tx3.at[r, d >> 1], rx3.at[r, plane], (r, 4), plane_peer(d)).start()

    def local_part(r, vector, parts):
        part = nugget[...] * vector + joined(dot(parts, kernel[...]))
        copy(tx0.at[r], rx0.at[r], (r, 0), plane_peer(1)).wait_recv()
        return part + joined(dot(split(rx0[r]), left_fine[0]))

    def end_round(r, count):
        slots = rx3.at[r, pl.ds(0, 31)]
        copy(slots, slots, (r, 4), plane_peer(1)).wait_recv()
        turned = rx3[r].reshape(256, 128).T
        sibling = jnp.concatenate([turned[:48], turned[48:96]], 1)
        far = joined(dot(split(sibling), order_left[...]))
        spare = turned[96:]
        return far, [
            jnp.concatenate(
                [spare[:, 16 * i : 16 * i + 1], spare[16:, 16 * i + 8 : 16 * i + 9]], 0
            ) * (1.0 / TOTAL)
            for i in range(count)
        ]

    first = right_sides[...]
    parts = start_round(0, first, [total_of(first * first)])

    order_left[...] = dot(order, levels_above(left_fine, left_coarse)).astype(BF16)
    c8[...] = jnp.zeros_like(c8)
    c8[0:3] = centres[...]
    coords = c8[...]
    c_high = coords.astype(BF16).astype(F32)
    c_mid = (coords - c_high).astype(BF16).astype(F32)
    c_low = coords - c_high - c_mid
    chosen = jnp.where(row == leaf_order[...], 1.0, 0.0).astype(BF16)
    split_coords = jnp.concatenate([c_high, c_mid, c_low, jnp.zeros_like(coords)], 0)
    picked = dot(split_coords.astype(BF16), chosen)
    points = (picked[0:8] + picked[8:16]) + picked[16:24]
    points_t = jnp.concatenate([points, jnp.zeros((120, ROWS), F32)], 0).T
    block = 64
    for start in range(0, ROWS, block):
        distance = jnp.full((block, ROWS), SHAPE_SQUARED, F32)
        for coord in range(3):
            between = points_t[start : start + block, coord : coord + 1] - points[coord : coord + 1]
            distance = distance + between * between
        kernel[start : start + block] = (jnp.sqrt(distance) * (1.0 / ROWS**0.5)).astype(BF16)

    near = local_part(0, first, parts)
    sums_round(0)
    far, (square,) = end_round(0, 1)
    norm = jnp.sqrt(square + EPSILON)
    basis = [first / norm]
    images = [(near + far) / norm]
    gram = [[square / (square + EPSILON)]]
    lanes = lax.broadcasted_iota(jnp.int32, (NRHS, 128), 1)
    table = jnp.zeros((NRHS, 128), F32)

    def orthogonalize(step, dots):
        coeffs, square = dots[:-1], dots[-1]
        count = len(coeffs)
        spread = [sum(gram[i][k] * coeffs[k] for k in range(count)) for i in range(count)]
        for i in range(count):
            square = square - coeffs[i] * (2.0 * coeffs[i] - spread[i])
        square = jnp.maximum(square, 0.0)
        norm = jnp.sqrt(square + EPSILON)
        column = [(coeffs[i] - spread[i]) / norm for i in range(count)]
        for i in range(count):
            gram[i].append(column[i])
        gram.append(column + [square / (square + EPSILON)])
        return coeffs, norm

    def combine(value, coeffs, earlier, norm):
        for coeff, other in zip(coeffs, earlier):
            value = value - coeff * other
        return value / norm

    def record(table, step, coeffs, norm):
        for i, value in enumerate(coeffs + [norm]):
            table = jnp.where(lanes == i * STEPS + step, value, table)
        return table

    for r in range(1, STEPS):
        image = images[-1]
        dots = [total_of(other * image) for other in basis] + [total_of(image * image)]
        parts = start_round(r, image, dots)
        near = local_part(r, image, parts)
        sums_round(r)
        far, dots = end_round(r, len(dots))
        coeffs, norm = orthogonalize(r - 1, dots)
        table = record(table, r - 1, coeffs, norm)
        basis.append(combine(image, coeffs, basis, norm))
        images.append(combine(near + far, coeffs, images, norm))

    image = images[-1]
    dots = [total_of(other * image) for other in basis] + [total_of(image * image)]
    side = jnp.zeros((128, 128), F32)
    lanes_all = lax.broadcasted_iota(jnp.int32, (128, 128), 1)
    zeros = jnp.zeros((32, 1), F32)
    for i in range(3):
        below = dots[2 * i + 1] if i < 2 else jnp.zeros((NRHS, 1), F32)
        side = jnp.where(lanes_all == i, jnp.concatenate([dots[2 * i], below, zeros], 0), side)
    tx4[...] = side.T[:8]

    @pl.loop(1, SLICES)
    def _(d):
        copy(tx4, rx4.at[d], (STEPS, 0), plane_peer(d)).start()

    slots = rx4.at[pl.ds(1, 31)]
    copy(slots, slots, (STEPS, 0), plane_peer(1)).wait_recv()
    tx5[...] = tree([tx4[...]] + [rx4[d] for d in range(1, SLICES)])

    @pl.loop(1, DEPTH)
    def _(z):
        copy(tx5, rx5.at[z], (STEPS, 1), depth_peer(z)).start()

    slots = rx5.at[pl.ds(1, 15)]
    copy(slots, slots, (STEPS, 1), depth_peer(1)).wait_recv()
    summed = tree([tx5[...]] + [rx5[z] for z in range(1, DEPTH)]) * (1.0 / TOTAL)
    side = jnp.concatenate([summed, jnp.zeros((120, 128), F32)], 0).T
    dots = [side[48 * (i % 2) : 48 * (i % 2) + 48, i // 2 : i // 2 + 1] for i in range(5)]
    coeffs, norm = orthogonalize(STEPS - 1, dots)
    hess[...] = record(table, STEPS - 1, coeffs, norm)
    out[...] = combine(image, coeffs, basis, norm)

    for r in range(STEPS):
        copy(tx0.at[r], rx0.at[r], (r, 0), plane_peer(1)).wait_send()
        copy(tx1.at[r, pl.ds(1, 31)], rx1.at[r, pl.ds(1, 31)], (r, 1), plane_peer(1)).wait_send()
        rows = rx2.at[r, pl.ds(2, 14)]
        copy(rows, rows, (r, 2), depth_peer(1)).wait_send()
        copy(txp.at[r], rxp.at[r], (r, 3), depth_peer(1)).wait_send()
        slots = rx3.at[r, pl.ds(0, 31)]
        copy(slots, slots, (r, 4), plane_peer(1)).wait_send()
    slots = rx4.at[pl.ds(1, 31)]
    copy(slots, slots, (STEPS, 0), plane_peer(1)).wait_send()
    slots = rx5.at[pl.ds(1, 15)]
    copy(slots, slots, (STEPS, 1), depth_peer(1)).wait_send()


def on_device(
    centres, leaf_order, nugget, left_fine, right_fine, left_coarse, right_coarse, right_sides
):
    vmem = pl.BlockSpec(memory_space=pltpu.VMEM)
    basis, table = pl.pallas_call(
        body,
        out_shape=(
            jax.ShapeDtypeStruct((NRHS, ROWS), F32),
            jax.ShapeDtypeStruct((NRHS, 128), F32),
        ),
        in_specs=[vmem] * 8,
        out_specs=(vmem, vmem),
        scratch_shapes=[
            pltpu.VMEM((8, ROWS), F32),
            pltpu.VMEM((512, ROWS), BF16),
            pltpu.VMEM((512, ROWS), BF16),
            pltpu.VMEM((ROWS, ROWS), BF16),
            pltpu.VMEM((STEPS, NRHS, RANK), F32),
            pltpu.VMEM((STEPS, NRHS, RANK), F32),
            pltpu.VMEM((STEPS, SLICES, 8, 128), F32),
            pltpu.VMEM((STEPS, SLICES, 8, 128), F32),
            pltpu.VMEM((STEPS, 3, 1, 128), F32),
            pltpu.VMEM((STEPS, DEPTH, 1, 128), F32),
            pltpu.VMEM((STEPS, 2, 8, 128), F32),
            pltpu.VMEM((STEPS, 2, 8, 128), F32),
            pltpu.VMEM((STEPS, 16, 8, 128), F32),
            pltpu.VMEM((STEPS, SLICES, 8, 128), F32),
            pltpu.VMEM((8, 128), F32),
            pltpu.VMEM((SLICES, 8, 128), F32),
            pltpu.VMEM((8, 128), F32),
            pltpu.VMEM((DEPTH, 8, 128), F32),
            pltpu.SemaphoreType.DMA((STEPS + 1, 5)),
            pltpu.SemaphoreType.DMA((STEPS + 1, 5)),
        ],
        compiler_params=pltpu.CompilerParams(
            collective_id=0, has_side_effects=True, vmem_limit_bytes=40 * 1024 * 1024
        ),
    )(
        centres, leaf_order, nugget.reshape(1, ROWS), left_fine, right_fine, left_coarse,
        right_coarse, right_sides,
    )
    hessenberg = table[:, : (STEPS + 1) * STEPS].reshape(NRHS, STEPS + 1, STEPS)
    return (basis, hessenberg)


def solution(mesh):
    return jax.shard_map(
        on_device,
        mesh=mesh,
        in_specs=(
            P(None, ("outer", "inner")),
            P(("outer", "inner"), None),
            P(("outer", "inner")),
            P(None, None, ("outer", "inner")),
            P(None, None, ("outer", "inner")),
            P(None, None, ("outer", "inner")),
            P(None, None, ("outer", "inner")),
            P(None, ("outer", "inner")),
        ),
        out_specs=(P(None, ("outer", "inner")), P()),
        check_vma=False,
    )
```

time: 1240 us -> 111 us (0.09)
  blocking collectives: 926 us -> 0 us
  starting transfers between devices: 182 us -> 0 us
  waiting for transfers between devices: 103 us -> 0 us
  Pallas kernels: 0 us -> 102 us
    psum x9 -> x0, blocking collectives: 926 us -> none  [the longest x4 417 us: on_device(): coeffs = lax.psum(local_products, ('inner', 'outer')) / total]
    ppermute x52 -> x0, starting transfers between devices: 182 us -> none  [partner(): lax.ppermute(value, axis, [(i, i ^ 1 << stride) for i in range(lax.axis_s...]
    ppermute x52 -> x0, waiting for transfers between devices: 103 us -> none  [partner(): lax.ppermute(value, axis, [(i, i ^ 1 << stride) for i in range(lax.axis_s...]
    pallas_call x0 -> x1, Pallas kernels: none -> 102 us  [on_device(): pl.pallas_call(body, out_shape=(jax.ShapeDtypeStruct((NRHS, ROWS), F32),...]
  transfers between devices with their start and end apart: 52 -> 0, of which waited for: 26 -> 0; matrix products, arithmetic and copies ran while one was open for 1% -> 0% of each run, Pallas kernels for 0% -> 0%
where the time goes in v1:
time: 111 us
  Pallas kernels  102 us (92%)
  local copies, waits for them, and re-layouts  8.12 us (7%)
    pallas_call x1, Pallas kernels, on_device(): pl.pallas_call(body, out_shape=(jax.ShapeDtypeStruct((NRHS, ROWS), F32),...  102 us
    unnamed x17, local copies, waits for them, and re-layouts  7.43 us

profile of v1, /device:TPU:1, one launch (start us, length us, event | category | flops | bytes accessed | tf_op | source)
XLA Modules:
  0.0 110.8 jit_solution(7717737025957453079)
XLA Ops:
  0.6 0.0 copy-start
  0.6 1.0 copy-done
  1.6 0.0 copy-start.1
  1.6 1.0 copy-done.1
  2.6 0.0 copy-start.2
  2.6 0.9 copy-done.2
  3.5 0.0 copy-start.3
  3.5 0.9 copy-done.3
  4.5 0.0 copy-start.4
  4.5 0.9 copy-done.4
  5.4 0.0 copy-start.5
  5.4 0.7 copy-done.5
  6.1 0.0 copy-start.6
  6.1 0.7 copy-done.6
  6.8 0.0 copy-start.7
  6.8 0.7 copy-done.7
  7.4 102.0 %shard_map.95 = (f32[48,512]{1,0:T(8,128)S(1)}, f32[48,128]{1,0:T(8,128)S(1)}) custom-call(f32[3,512]{1,0:T(4,128)S(1)} %copy-done.5, s32[1,512]{1,0:T(1,128)S(1)} %copy-done.6, f32[1,512]{1,0:T(1,128)S(1)} %bitcast.5, bf16[4,64,512]{2,1,0:T(8,128)(2,1)S(1)} %copy-done.2, bf16[4,64,512]{2,1,0:T(8,128)(2,1)S(1)} %copy-done.3, ...), custom_call_target="tpu_custom_call" | custom-call | tf_op jit(solution)/shard_map/pallas_call | solution.py:311
  109.5 0.1 copy.11
  109.5 0.6 reshape.11
  110.2 0.6 copy.13
Async XLA Ops:
  0.6 1.0 copy-start
  1.6 1.0 copy-start.1
  2.6 0.9 copy-start.2
  3.5 0.9 copy-start.3
  4.5 0.9 copy-start.4
  5.4 0.7 copy-start.5
  6.1 0.7 copy-start.6
  6.8 0.7 copy-start.7

commit v2 on v1

--- a/solution.py
+++ b/solution.py
@@ -50,12 +50,20 @@
     return values[0]
 
 
-def body(
-    centres, leaf_order, nugget, left_fine, right_fine, left_coarse, right_coarse, right_sides,
-    out, hess,
-    c8, order_right, order_left, kernel, tx0, rx0, tx1, rx1, tx2, rx2, txp, rxp, tx3, rx3,
-    tx4, rx4, tx5, rx5, send, recv,
-):
+def body(*refs):
+    sources, refs = refs[:8], refs[8:]
+    out, hess = refs[:2]
+    held, refs = refs[2:10], refs[10:]
+    centres, leaf_order, nugget, left_fine, right_fine, left_coarse, right_coarse, right_sides = held
+    (
+        c8, order_right, order_left, kernel, tx0, rx0, tx1, rx1, tx2, rx2, txp, rxp, tx3, rx3,
+        tx4, rx4, tx5, rx5, send, recv, fetched,
+    ) = refs
+    fetches = [
+        pltpu.make_async_copy(sources[i], held[i], fetched.at[i]) for i in range(8)
+    ]
+    for i in (4, 6, 7, 3, 5, 1, 0, 2):
+        fetches[i].start()
     inner, outer = lax.axis_index("inner"), lax.axis_index("outer")
     plane = (outer % 4) * 8 + inner % 8
 
@@ -91,7 +99,9 @@
             [fine[1:].reshape(3 * RANK, ROWS), coarse[...].reshape(5 * RANK, ROWS)], 0
         )
 
-    order_right[...] = dot(order, levels_above(right_fine, right_coarse)).astype(BF16)
+    fetches[4].wait()
+    fetches[6].wait()
+    order_right[...] = dot(order, levels_above(right_fine, right_coarse)).T.astype(BF16)
 
     lane = lax.broadcasted_iota(jnp.int32, (32, 256), 1)
     spare_dot, spare_odd = (lane >> 4) & 7, ((lane >> 3) & 1) == 1
@@ -100,7 +110,7 @@
 
     def start_round(r, vector, dots):
         parts = split(vector)
-        terms = joined(dot_t(parts, order_right[...]))
+        terms = joined(dot(parts, order_right[...]))
         spare = jnp.zeros((32, 256), F32)
         for i, value in enumerate(dots):
             spare = jnp.where(
@@ -109,10 +119,9 @@
         tiles = jnp.concatenate([terms[:, :256], terms[:, 256:], spare], 0).T
         tx1[r] = tiles.reshape(SLICES, 8, 128)
         if r == 0:
+            prepare()
             pl.semaphore_wait(barrier, SLICES + DEPTH - 2)
-
-        @pl.loop(1, SLICES)
-        def _(d):
+        for d in range(SLICES - 1, 0, -1):
             copy(tx1.at[r, plane ^ d], rx1.at[r, d], (r, 1), plane_peer(d)).start()
 
         tx0[r] = joined(dot_t(parts, right_fine[0]))
@@ -135,9 +144,8 @@
             )
         copy(txp.at[r], rxp.at[r], (r, 3), depth_peer(1)).start()
 
-        @pl.loop(2, DEPTH)
-        def _(z):
-            which = jnp.where(z < 4, 0, jnp.where(z < 8, 1, 2))
+        for z in range(DEPTH - 1, 1, -1):
+            which = 0 if z < 4 else 1 if z < 8 else 2
             copy(tx2.at[r, which], rx2.at[r, z], (r, 2), depth_peer(z)).start()
 
         copy(txp.at[r], rxp.at[r], (r, 3), depth_peer(1)).wait_recv()
@@ -167,8 +175,7 @@
                 if e == 0:
                     rx3[r, plane] = tile
 
-        @pl.loop(1, SLICES)
-        def _(d):
+        for d in range(SLICES - 1, 0, -1):
             copy(tx3.at[r, d >> 1], rx3.at[r, plane], (r, 4), plane_peer(d)).start()
 
     def local_part(r, vector, parts):
@@ -190,12 +197,17 @@
             for i in range(count)
         ]
 
+    def prepare():
+        for i in (0, 1, 2, 3, 5):
+            fetches[i].wait()
+        order_left[...] = dot(order, levels_above(left_fine, left_coarse)).astype(BF16)
+        c8[...] = jnp.zeros_like(c8)
+        c8[0:3] = centres[...]
+
+    fetches[7].wait()
     first = right_sides[...]
     parts = start_round(0, first, [total_of(first * first)])
 
-    order_left[...] = dot(order, levels_above(left_fine, left_coarse)).astype(BF16)
-    c8[...] = jnp.zeros_like(c8)
-    c8[0:3] = centres[...]
     coords = c8[...]
     c_high = coords.astype(BF16).astype(F32)
     c_mid = (coords - c_high).astype(BF16).astype(F32)
@@ -269,16 +281,14 @@
         side = jnp.where(lanes_all == i, jnp.concatenate([dots[2 * i], below, zeros], 0), side)
     tx4[...] = side.T[:8]
 
-    @pl.loop(1, SLICES)
-    def _(d):
+    for d in range(SLICES - 1, 0, -1):
         copy(tx4, rx4.at[d], (STEPS, 0), plane_peer(d)).start()
 
     slots = rx4.at[pl.ds(1, 31)]
     copy(slots, slots, (STEPS, 0), plane_peer(1)).wait_recv()
     tx5[...] = tree([tx4[...]] + [rx4[d] for d in range(1, SLICES)])
 
-    @pl.loop(1, DEPTH)
-    def _(z):
+    for z in range(DEPTH - 1, 0, -1):
         copy(tx5, rx5.at[z], (STEPS, 1), depth_peer(z)).start()
 
     slots = rx5.at[pl.ds(1, 15)]
@@ -308,15 +318,19 @@
     centres, leaf_order, nugget, left_fine, right_fine, left_coarse, right_coarse, right_sides
 ):
     vmem = pl.BlockSpec(memory_space=pltpu.VMEM)
+    arguments = (
+        centres, leaf_order, nugget.reshape(1, ROWS), left_fine, right_fine, left_coarse,
+        right_coarse, right_sides,
+    )
     basis, table = pl.pallas_call(
         body,
         out_shape=(
             jax.ShapeDtypeStruct((NRHS, ROWS), F32),
             jax.ShapeDtypeStruct((NRHS, 128), F32),
         ),
-        in_specs=[vmem] * 8,
+        in_specs=[pl.BlockSpec(memory_space=pl.ANY)] * 8,
         out_specs=(vmem, vmem),
-        scratch_shapes=[
+        scratch_shapes=[pltpu.VMEM(value.shape, value.dtype) for value in arguments] + [
             pltpu.VMEM((8, ROWS), F32),
             pltpu.VMEM((512, ROWS), BF16),
             pltpu.VMEM((512, ROWS), BF16),
@@ -337,14 +351,12 @@
             pltpu.VMEM((DEPTH, 8, 128), F32),
             pltpu.SemaphoreType.DMA((STEPS + 1, 5)),
             pltpu.SemaphoreType.DMA((STEPS + 1, 5)),
+            pltpu.SemaphoreType.DMA((8,)),
         ],
         compiler_params=pltpu.CompilerParams(
-            collective_id=0, has_side_effects=True, vmem_limit_bytes=40 * 1024 * 1024
+            collective_id=0, has_side_effects=True, vmem_limit_bytes=60 * 1024 * 1024
         ),
-    )(
-        centres, leaf_order, nugget.reshape(1, ROWS), left_fine, right_fine, left_coarse,
-        right_coarse, right_sides,
-    )
+    )(*arguments)
     hessenberg = table[:, : (STEPS + 1) * STEPS].reshape(NRHS, STEPS + 1, STEPS)
     return (basis, hessenberg)
 

time: 111 us -> 103 us (0.928)
  local copies, waits for them, and re-layouts: 8.12 us -> 2.97 us
  Pallas kernels: 102 us -> 98.9 us
    unnamed x17 -> x1, local copies, waits for them, and re-layouts: 7.43 us -> 1.54 us
    pallas_call x1, Pallas kernels: 102 us -> 98.9 us  [on_device(): pl.pallas_call(body, out_shape=(jax.ShapeDtypeStruct((NRHS, ROWS), F32),...]
where the time goes in v2:
time: 103 us
  Pallas kernels  98.9 us (96%)
  local copies, waits for them, and re-layouts  2.97 us (3%)
    pallas_call x1, Pallas kernels, on_device(): pl.pallas_call(body, out_shape=(jax.ShapeDtypeStruct((NRHS, ROWS), F32),...  98.9 us

profile of v2, /device:TPU:1, one launch (start us, length us, event | category | flops | bytes accessed | tf_op | source)
XLA Modules:
  0.0 102.6 jit_solution(7722128786503765732)
XLA Ops:
  0.6 98.9 %shard_map.95 = (f32[48,512]{1,0:T(8,128)}, f32[48,128]{1,0:T(8,128)}) custom-call(f32[3,512]{1,0:T(4,128)} %refs_0_.1, s32[1,512]{1,0:T(1,128)} %refs_1_.1, f32[1,512]{1,0:T(1,128)} %bitcast.5, bf16[4,64,512]{2,1,0:T(8,128)(2,1)} %refs_3_.1, bf16[4,64,512]{2,1,0:T(8,128)(2,1)} %refs_4_.1, bf16[5,64,512]{2,1,0:T(8,128)(2,1)} %refs_5_.1, ...), custom_call_target="tpu_custom_call" | custom-call | tf_op jit(solution)/shard_map/pallas_call | solution.py:325
  99.6 0.8 copy.11
  100.4 0.6 reshape.11
  101.0 1.5 %copy.13 = f32[48,512]{1,0:T(8,128)} copy(f32[48,512]{1,0:T(8,128)} %get-tuple-element.10) | data formatting | bytes 196608

commit v3 on v2

--- a/solution.py
+++ b/solution.py
@@ -52,8 +52,8 @@
 
 def body(*refs):
     sources, refs = refs[:8], refs[8:]
-    out, hess = refs[:2]
-    held, refs = refs[2:10], refs[10:]
+    both = refs[0]
+    held, refs = refs[1:9], refs[9:]
     centres, leaf_order, nugget, left_fine, right_fine, left_coarse, right_coarse, right_sides = held
     (
         c8, order_right, order_left, kernel, tx0, rx0, tx1, rx1, tx2, rx2, txp, rxp, tx3, rx3,
@@ -81,13 +81,10 @@
 
     barrier = pltpu.get_barrier_semaphore()
 
-    @pl.loop(1, SLICES)
-    def _(d):
+    for z in range(1, DEPTH):
+        pl.semaphore_signal(barrier, inc=1, device_id=depth_peer(z), device_id_type=MESH)
+    for d in range(SLICES - 1, 0, -1):
         pl.semaphore_signal(barrier, inc=1, device_id=plane_peer(d), device_id_type=MESH)
-
-    @pl.loop(1, DEPTH)
-    def _(z):
-        pl.semaphore_signal(barrier, inc=1, device_id=depth_peer(z), device_id_type=MESH)
 
     row = lax.broadcasted_iota(jnp.int32, (512, 512), 0)
     col = lax.broadcasted_iota(jnp.int32, (512, 512), 1)
@@ -138,10 +135,11 @@
         whole = half[0] + half[1]
         for z in range(3):
             tx2[r, z] = whole[5 + z : 6 + z]
+        for y in range(4):
+            txp[r, y] = line[y][2:3]
+            txp[r, 4 + y] = line[y][3:4]
         for m in range(2):
-            txp[r, m] = jnp.where(
-                tile_row < 5, line[2 * m], pltpu.roll(line[2 * m + 1], 3, axis=0)
-            )
+            txp[r, 8 + m] = half[m][4:5]
         copy(txp.at[r], rxp.at[r], (r, 3), depth_peer(1)).start()
 
         for z in range(DEPTH - 1, 1, -1):
@@ -151,21 +149,16 @@
         copy(txp.at[r], rxp.at[r], (r, 3), depth_peer(1)).wait_recv()
         rows = rx2.at[r, pl.ds(2, 14)]
         copy(rows, rows, (r, 2), depth_peer(1)).wait_recv()
-        far = []
-        for m in range(2):
-            both = rxp[r, m]
-            far += [both, pltpu.roll(both, 5, axis=0)]
-        far_half = [far[0] + far[1], far[2] + far[3]]
         six = tree([rx2[r, z] for z in range(2, 4)])
         seven = tree([rx2[r, z] for z in range(4, 8)])
         eight = tree([rx2[r, z] for z in range(8, 16)])
-        products = whole[2:3] + (far_half[0] + far_half[1])[2:3]
+        products = whole[2:3] + tree([rxp[r, y] for y in range(4)])
         products = products + six + seven + eight
         high = jnp.where(tile_row == 5, six, jnp.where(tile_row == 6, seven, eight))
         for y in range(4):
-            base = jnp.where(tile_row == 4, half[1 - y // 2] + far_half[1 - y // 2], high)
-            base = jnp.where(tile_row == 3, line[y ^ 1] + far[y ^ 1], base)
-            base = jnp.where(tile_row == 2, far[y], base)
+            base = jnp.where(tile_row == 4, half[1 - y // 2] + rxp[r, 9 - y // 2], high)
+            base = jnp.where(tile_row == 3, line[y ^ 1] + rxp[r, 4 + (y ^ 1)], base)
+            base = jnp.where(tile_row == 2, rxp[r, y], base)
             for x in range(4):
                 e = 4 * y + x
                 tile = jnp.where(tile_row == 1, pair[(e // 2) ^ 1], base)
@@ -228,9 +221,9 @@
     near = local_part(0, first, parts)
     sums_round(0)
     far, (square,) = end_round(0, 1)
-    norm = jnp.sqrt(square + EPSILON)
-    basis = [first / norm]
-    images = [(near + far) / norm]
+    scale = 1.0 / jnp.sqrt(square + EPSILON)
+    basis = [first * scale]
+    images = [(near + far) * scale]
     gram = [[square / (square + EPSILON)]]
     lanes = lax.broadcasted_iota(jnp.int32, (NRHS, 128), 1)
     table = jnp.zeros((NRHS, 128), F32)
@@ -243,16 +236,17 @@
             square = square - coeffs[i] * (2.0 * coeffs[i] - spread[i])
         square = jnp.maximum(square, 0.0)
         norm = jnp.sqrt(square + EPSILON)
-        column = [(coeffs[i] - spread[i]) / norm for i in range(count)]
+        scale = 1.0 / norm
+        column = [(coeffs[i] - spread[i]) * scale for i in range(count)]
         for i in range(count):
             gram[i].append(column[i])
         gram.append(column + [square / (square + EPSILON)])
-        return coeffs, norm
-
-    def combine(value, coeffs, earlier, norm):
+        return coeffs, norm, scale
+
+    def combine(value, coeffs, earlier, scale):
         for coeff, other in zip(coeffs, earlier):
             value = value - coeff * other
-        return value / norm
+        return value * scale
 
     def record(table, step, coeffs, norm):
         for i, value in enumerate(coeffs + [norm]):
@@ -266,10 +260,10 @@
         near = local_part(r, image, parts)
         sums_round(r)
         far, dots = end_round(r, len(dots))
-        coeffs, norm = orthogonalize(r - 1, dots)
+        coeffs, norm, scale = orthogonalize(r - 1, dots)
         table = record(table, r - 1, coeffs, norm)
-        basis.append(combine(image, coeffs, basis, norm))
-        images.append(combine(near + far, coeffs, images, norm))
+        basis.append(combine(image, coeffs, basis, scale))
+        images.append(combine(near + far, coeffs, images, scale))
 
     image = images[-1]
     dots = [total_of(other * image) for other in basis] + [total_of(image * image)]
@@ -279,7 +273,7 @@
     for i in range(3):
         below = dots[2 * i + 1] if i < 2 else jnp.zeros((NRHS, 1), F32)
         side = jnp.where(lanes_all == i, jnp.concatenate([dots[2 * i], below, zeros], 0), side)
-    tx4[...] = side.T[:8]
+    tx4[...] = side.T[:4]
 
     for d in range(SLICES - 1, 0, -1):
         copy(tx4, rx4.at[d], (STEPS, 0), plane_peer(d)).start()
@@ -294,11 +288,11 @@
     slots = rx5.at[pl.ds(1, 15)]
     copy(slots, slots, (STEPS, 1), depth_peer(1)).wait_recv()
     summed = tree([tx5[...]] + [rx5[z] for z in range(1, DEPTH)]) * (1.0 / TOTAL)
-    side = jnp.concatenate([summed, jnp.zeros((120, 128), F32)], 0).T
+    side = jnp.concatenate([summed, jnp.zeros((124, 128), F32)], 0).T
     dots = [side[48 * (i % 2) : 48 * (i % 2) + 48, i // 2 : i // 2 + 1] for i in range(5)]
-    coeffs, norm = orthogonalize(STEPS - 1, dots)
-    hess[...] = record(table, STEPS - 1, coeffs, norm)
-    out[...] = combine(image, coeffs, basis, norm)
+    coeffs, norm, scale = orthogonalize(STEPS - 1, dots)
+    both[:, ROWS:] = record(table, STEPS - 1, coeffs, norm)
+    both[:, :ROWS] = combine(image, coeffs, basis, scale)
 
     for r in range(STEPS):
         copy(tx0.at[r], rx0.at[r], (r, 0), plane_peer(1)).wait_send()
@@ -322,14 +316,11 @@
         centres, leaf_order, nugget.reshape(1, ROWS), left_fine, right_fine, left_coarse,
         right_coarse, right_sides,
     )
-    basis, table = pl.pallas_call(
+    both = pl.pallas_call(
         body,
-        out_shape=(
-            jax.ShapeDtypeStruct((NRHS, ROWS), F32),
-            jax.ShapeDtypeStruct((NRHS, 128), F32),
-        ),
+        out_shape=jax.ShapeDtypeStruct((NRHS, ROWS + 128), F32),
         in_specs=[pl.BlockSpec(memory_space=pl.ANY)] * 8,
-        out_specs=(vmem, vmem),
+        out_specs=vmem,
         scratch_shapes=[pltpu.VMEM(value.shape, value.dtype) for value in arguments] + [
             pltpu.VMEM((8, ROWS), F32),
             pltpu.VMEM((512, ROWS), BF16),
@@ -341,14 +332,14 @@
             pltpu.VMEM((STEPS, SLICES, 8, 128), F32),
             pltpu.VMEM((STEPS, 3, 1, 128), F32),
             pltpu.VMEM((STEPS, DEPTH, 1, 128), F32),
-            pltpu.VMEM((STEPS, 2, 8, 128), F32),
-            pltpu.VMEM((STEPS, 2, 8, 128), F32),
+            pltpu.VMEM((STEPS, 10, 1, 128), F32),
+            pltpu.VMEM((STEPS, 10, 1, 128), F32),
             pltpu.VMEM((STEPS, 16, 8, 128), F32),
             pltpu.VMEM((STEPS, SLICES, 8, 128), F32),
-            pltpu.VMEM((8, 128), F32),
-            pltpu.VMEM((SLICES, 8, 128), F32),
-            pltpu.VMEM((8, 128), F32),
-            pltpu.VMEM((DEPTH, 8, 128), F32),
+            pltpu.VMEM((4, 128), F32),
+            pltpu.VMEM((SLICES, 4, 128), F32),
+            pltpu.VMEM((4, 128), F32),
+            pltpu.VMEM((DEPTH, 4, 128), F32),
             pltpu.SemaphoreType.DMA((STEPS + 1, 5)),
             pltpu.SemaphoreType.DMA((STEPS + 1, 5)),
             pltpu.SemaphoreType.DMA((8,)),
@@ -357,8 +348,8 @@
             collective_id=0, has_side_effects=True, vmem_limit_bytes=60 * 1024 * 1024
         ),
     )(*arguments)
-    hessenberg = table[:, : (STEPS + 1) * STEPS].reshape(NRHS, STEPS + 1, STEPS)
-    return (basis, hessenberg)
+    table = both[:, ROWS : ROWS + (STEPS + 1) * STEPS]
+    return (both[:, :ROWS], table.reshape(NRHS, STEPS + 1, STEPS))
 
 
 def solution(mesh):

time: 103 us -> 101 us (0.981)
    unnamed x1 -> x0, local copies, waits for them, and re-layouts: 1.54 us -> none
where the time goes in v3:
time: 101 us
  Pallas kernels  98.1 us (97%)
  local copies, waits for them, and re-layouts  2.24 us (2%)
    pallas_call x1, Pallas kernels, on_device(): pl.pallas_call(body, out_shape=jax.ShapeDtypeStruct((NRHS, ROWS + 128), F...  98.1 us

profile of v3, /device:TPU:1, one launch (start us, length us, event | category | flops | bytes accessed | tf_op | source)
XLA Modules:
  0.0 101.0 jit_solution(18411387385386603537)
XLA Ops:
  0.6 98.1 %shard_map.95 = f32[48,640]{1,0:T(8,128)} custom-call(f32[3,512]{1,0:T(4,128)} %refs_0_.1, s32[1,512]{1,0:T(1,128)} %refs_1_.1, f32[1,512]{1,0:T(1,128)} %bitcast.3, bf16[4,64,512]{2,1,0:T(8,128)(2,1)} %refs_3_.1, bf16[4,64,512]{2,1,0:T(8,128)(2,1)} %refs_4_.1, bf16[5,64,512]{2,1,0:T(8,128)(2,1)} %refs_5_.1, bf16[5,64,512]{2,1,0:T(8,128)(2,1)} %refs_6_.1, ...), custom_call_target="tpu_custom_call" | custom-call | tf_op jit(solution)/shard_map/pallas_call | solution.py:319
  98.8 0.0 slice-start
  98.8 1.5 %slice.6 = f32[48,512]{1,0:T(8,128)} slice(f32[48,640]{1,0:T(8,128)} %shard_map.95), slice={[0:48], [0:512]} | slice | bytes 196608 | tf_op jit(solution)/shard_map/slice | solution.py:352
  100.3 0.0 slice-done
  100.3 0.1 copy.11
  100.4 0.6 reshape.11
Async XLA Ops:
  98.8 1.6 %slice-start = ((f32[48,640]{1,0:T(8,128)}), f32[48,20]{1,0:T(8,128)S(1)}, s32[]{:S(2)}) async-start(f32[48,640]{1,0:T(8,128)} %shard_map.95), calls=%async_computation | async-start | bytes 49152 | tf_op jit(solution)/shard_map/slice | solution.py:351

commit v4 on v3

--- a/solution.py
+++ b/solution.py
@@ -132,20 +132,21 @@
         pair = [chip[2 * h] + chip[2 * h + 1] for h in range(8)]
         line = [pair[2 * y] + pair[2 * y + 1] for y in range(4)]
         half = [line[0] + line[1], line[2] + line[3]]
-        whole = half[0] + half[1]
-        for z in range(3):
-            tx2[r, z] = whole[5 + z : 6 + z]
         for y in range(4):
             txp[r, y] = line[y][2:3]
             txp[r, 4 + y] = line[y][3:4]
         for m in range(2):
             txp[r, 8 + m] = half[m][4:5]
         copy(txp.at[r], rxp.at[r], (r, 3), depth_peer(1)).start()
-
+        whole = half[0] + half[1]
+        for z in range(3):
+            tx2[r, z] = whole[5 + z : 6 + z]
         for z in range(DEPTH - 1, 1, -1):
             which = 0 if z < 4 else 1 if z < 8 else 2
             copy(tx2.at[r, which], rx2.at[r, z], (r, 2), depth_peer(z)).start()
 
+        lows = [jnp.where(tile_row == 0, chip[e ^ 1], pair[(e // 2) ^ 1]) for e in range(16)]
+        low = (tile_row < 2) & ~tile_spare
         copy(txp.at[r], rxp.at[r], (r, 3), depth_peer(1)).wait_recv()
         rows = rx2.at[r, pl.ds(2, 14)]
         copy(rows, rows, (r, 2), depth_peer(1)).wait_recv()
@@ -155,21 +156,19 @@
         products = whole[2:3] + tree([rxp[r, y] for y in range(4)])
         products = products + six + seven + eight
         high = jnp.where(tile_row == 5, six, jnp.where(tile_row == 6, seven, eight))
-        for y in range(4):
+        for y in range(3, -1, -1):
             base = jnp.where(tile_row == 4, half[1 - y // 2] + rxp[r, 9 - y // 2], high)
             base = jnp.where(tile_row == 3, line[y ^ 1] + rxp[r, 4 + (y ^ 1)], base)
             base = jnp.where(tile_row == 2, rxp[r, y], base)
-            for x in range(4):
+            base = jnp.where(tile_spare, products, base)
+            for x in range(3, -1, -1):
                 e = 4 * y + x
-                tile = jnp.where(tile_row == 1, pair[(e // 2) ^ 1], base)
-                tile = jnp.where(tile_row == 0, chip[e ^ 1], tile)
-                tile = jnp.where(tile_spare, products, tile)
+                tile = jnp.where(low, lows[e], base)
                 tx3[r, e] = tile
                 if e == 0:
                     rx3[r, plane] = tile
-
-        for d in range(SLICES - 1, 0, -1):
-            copy(tx3.at[r, d >> 1], rx3.at[r, plane], (r, 4), plane_peer(d)).start()
+                for d in (2 * e + 1, 2 * e)[: 2 if e else 1]:
+                    copy(tx3.at[r, e], rx3.at[r, plane], (r, 4), plane_peer(d)).start()
 
     def local_part(r, vector, parts):
         part = nugget[...] * vector + joined(dot(parts, kernel[...]))

time: 101 us -> 101 us (level)
  no operation moved by 1% of the time
where the time goes in v4:
time: 101 us
  Pallas kernels  98.1 us (97%)
  local copies, waits for them, and re-layouts  2.24 us (2%)
    pallas_call x1, Pallas kernels, on_device(): pl.pallas_call(body, out_shape=jax.ShapeDtypeStruct((NRHS, ROWS + 128), F...  98.1 us

profile of v4, /device:TPU:1, one launch (start us, length us, event | category | flops | bytes accessed | tf_op | source)
XLA Modules:
  0.0 101.0 jit_solution(13450107763717886272)
XLA Ops:
  0.6 98.1 %shard_map.95 = f32[48,640]{1,0:T(8,128)} custom-call(f32[3,512]{1,0:T(4,128)} %refs_0_.1, s32[1,512]{1,0:T(1,128)} %refs_1_.1, f32[1,512]{1,0:T(1,128)} %bitcast.3, bf16[4,64,512]{2,1,0:T(8,128)(2,1)} %refs_3_.1, bf16[4,64,512]{2,1,0:T(8,128)(2,1)} %refs_4_.1, bf16[5,64,512]{2,1,0:T(8,128)(2,1)} %refs_5_.1, bf16[5,64,512]{2,1,0:T(8,128)(2,1)} %refs_6_.1, ...), custom_call_target="tpu_custom_call" | custom-call | tf_op jit(solution)/shard_map/pallas_call | solution.py:318
  98.8 0.0 slice-start
  98.8 1.5 %slice.6 = f32[48,512]{1,0:T(8,128)} slice(f32[48,640]{1,0:T(8,128)} %shard_map.95), slice={[0:48], [0:512]} | slice | bytes 196608 | tf_op jit(solution)/shard_map/slice | solution.py:351
  100.3 0.0 slice-done
  100.3 0.1 copy.11
  100.4 0.6 reshape.11
Async XLA Ops:
  98.8 1.6 %slice-start = ((f32[48,640]{1,0:T(8,128)}), f32[48,20]{1,0:T(8,128)S(1)}, s32[]{:S(2)}) async-start(f32[48,640]{1,0:T(8,128)} %shard_map.95), calls=%async_computation | async-start | bytes 49152 | tf_op jit(solution)/shard_map/slice | solution.py:350
